TPU v7x, 512 devices: a whole 4x4x16 slice. The times are simulated.
512 devices in a mesh: blk: 64 (over z_lo, x, core), rep: 8 (over y, z_hi).
Axes of the slice: x: 4, y: 4, z: 16 (z_hi: 2, z_lo: 8; z = z_hi * 8 + z_lo), core: 2. Of those that a mesh axis runs over, the one named last changes fastest.
Arguments:
- features: bfloat16 [32768, 128], P('blk'), may hold values from -6 to 6
- adjacency: bfloat16 [64, 8, 6, 512, 512], P('blk', 'rep'), may hold values from -0.0390625 to 0.0390625
- tile_column: int32 [64, 8, 6], P('blk', 'rep'), may hold values from -1 to 63, as said below
- weight: bfloat16 [128, 128], replicated, may hold values from -0.5 to 0.5
- out_bias: bfloat16 [128], replicated, may hold values from -3 to 3
Outputs:
- output: bfloat16 [32768, 128], P(('blk', 'rep'))
Inputs may be any that keep to these rules, and one draw needn't show every extreme that they name: `tile_column`: for row block b and replica r, each live slot holds a column block (b - r - 8 * t) mod 64 with t in 0 to 7; live columns of one device are distinct; live slots come first; each device has one or more live slots; some device has all 6 live.
All inputs are finite; a program needn't handle non-finite values.
Results may differ from a plain program's by a relative error of at most 0.0043.
Values may be sent and summed in bfloat16 or wider, within the bound.
No kernel may reach another device: no remote copies, remote signals or barrier semaphores. Data moves between devices by JAX's collectives and lax.ppermute only.
A program may use at most 64 MiB of HBM per device.

v0:
```python
import jax
import jax.numpy as jnp
from jax import lax
from jax.sharding import PartitionSpec as P


def passed_along(array, axis, by):
    peers = lax.axis_size(axis)
    return lax.ppermute(array, axis, [(i, (i + by) % peers) for i in range(peers)])


def local(features, adjacency, tile_column, weight, out_bias):
    replicas = lax.axis_size("rep")
    block_count = lax.axis_size("blk")
    section_count = block_count // replicas
    row_block = lax.axis_index("blk")
    replica = lax.axis_index("rep")
    columns = tile_column.reshape(-1)
    tile_set = adjacency.reshape(adjacency.shape[2:])
    slot_order = jnp.arange(columns.shape[0], dtype=jnp.int32)
    initial = features
    for bit_level in range(replicas.bit_length()):
        if 1 << bit_level >= replicas:
            break
        shifted = passed_along(initial, "blk", 1 << bit_level)
        initial = jnp.where(replica >> bit_level & 1 == 1, shifted, initial)
    running = jnp.zeros((features.shape[0], features.shape[1]), jnp.float32)
    arrived = initial
    for section_num in range(section_count):
        if section_num > 0:
            arrived = passed_along(arrived, "blk", replicas)
        wanted = jnp.mod(row_block - replica - replicas * section_num, block_count)
        matches = columns == wanted
        chosen = jnp.sum(jnp.where(matches, slot_order, 0))
        tile_now = lax.dynamic_index_in_dim(tile_set, chosen, 0, False)
        running = lax.cond(
            jnp.any(matches),
            lambda: running + jnp.dot(tile_now, arrived, preferred_element_type=jnp.float32),
            lambda: running,
        )
    row_count = features.shape[0] // replicas
    summed = lax.psum(running, "rep")
    owned_rows = lax.dynamic_slice_in_dim(summed, replica * row_count, row_count, 0)
    hidden = owned_rows.astype(jnp.bfloat16)
    result = jnp.dot(hidden, weight, preferred_element_type=jnp.float32) + out_bias.astype(
        jnp.float32
    )
    return jnp.maximum(result, 0.0).astype(jnp.bfloat16)


def solution(mesh):
    in_specs = (P("blk", None), P("blk", "rep", None, None, None), P("blk", "rep", None), P(), P())
    out_specs = P(("blk", "rep"), None)
    return jax.shard_map(local, mesh=mesh, in_specs=in_specs, out_specs=out_specs, check_vma=False)
```

profile of v0, /device:TPU:224, one launch (start us, length us, event | category | flops | bytes accessed | tf_op | source)
XLA Modules:
  0.0 251.8 jit_solution(1300861228709041578)
XLA Ops:
  0.0 0.0 copy-start
  0.0 2.0 collective-permute-start
  2.1 6.7 %collective-permute-done = bf16[512,128]{1,0:T(8,128)(2,1)S(1)} collective-permute-done((bf16[512,128]{1,0:T(8,128)(2,1)}, bf16[512,128]{1,0:T(8,128)(2,1)S(1)}, u32[]{:S(2)}, u32[]{:S(2)}) %collective-permute-start) | collective-permute-done | bytes 131104 | tf_op jit(solution)/shard_map/ppermute | solution.py:9
  8.7 0.9 broadcast_select_fusion
  9.7 1.9 collective-permute-start.1
  11.6 7.0 %collective-permute-done.1 = bf16[512,128]{1,0:T(8,128)(2,1)S(1)} collective-permute-done((bf16[512,128]{1,0:T(8,128)(2,1)S(1)}, bf16[512,128]{1,0:T(8,128)(2,1)S(1)}, u32[]{:S(2)}, u32[]{:S(2)}) %collective-permute-start.1) | collective-permute-done | bytes 131104 | tf_op jit(solution)/shard_map/ppermute | solution.py:9
  18.6 1.9 collective-permute-start.2
  20.6 7.3 %collective-permute-done.2 = bf16[512,128]{1,0:T(8,128)(2,1)S(1)} collective-permute-done((bf16[512,128]{1,0:T(8,128)(2,1)S(1)}, bf16[512,128]{1,0:T(8,128)(2,1)S(1)}, u32[]{:S(2)}, u32[]{:S(2)}) %collective-permute-start.2) | collective-permute-done | bytes 131104 | tf_op jit(solution)/shard_map/ppermute | solution.py:9
  27.9 24.5 %collective-permute-start.3 = (bf16[512,128]{1,0:T(8,128)(2,1)S(1)}, bf16[512,128]{1,0:T(8,128)(2,1)S(1)}, u32[]{:S(2)}, u32[]{:S(2)}) collective-permute-start(bf16[512,128]{1,0:T(8,128)(2,1)S(1)} %broadcast_select_fusion.2), channel_id=1, source_target_pairs={{0,64},{8,72},{16,80},{24,88},{32,96},{40,104},{48,112},{56,120},{... | collective-permute-start | bytes 393224 | tf_op jit(solution)/shard_map/ppermute | solution.py:9
  52.4 2.6 %collective-permute-done.3 = bf16[512,128]{1,0:T(8,128)(2,1)S(1)} collective-permute-done((bf16[512,128]{1,0:T(8,128)(2,1)S(1)}, bf16[512,128]{1,0:T(8,128)(2,1)S(1)}, u32[]{:S(2)}, u32[]{:S(2)}) %collective-permute-start.3) | collective-permute-done | bytes 131104 | tf_op jit(solution)/shard_map/ppermute | solution.py:9
  55.0 11.0 %collective-permute-start.4 = (bf16[512,128]{1,0:T(8,128)(2,1)S(1)}, bf16[512,128]{1,0:T(8,128)(2,1)S(1)}, u32[]{:S(2)}, u32[]{:S(2)}) collective-permute-start(bf16[512,128]{1,0:T(8,128)(2,1)S(1)} %collective-permute-done.3), channel_id=1, source_target_pairs={{0,64},{8,72},{16,80},{24,88},{32,96},{40,104},{48,112},{56,120},{... | collective-permute-start | bytes 393224 | tf_op jit(solution)/shard_map/ppermute | solution.py:9
  66.0 2.5 collective-permute-done.4
  68.5 10.9 %collective-permute-start.5 = (bf16[512,128]{1,0:T(8,128)(2,1)S(1)}, bf16[512,128]{1,0:T(8,128)(2,1)S(1)}, u32[]{:S(2)}, u32[]{:S(2)}) collective-permute-start(bf16[512,128]{1,0:T(8,128)(2,1)S(1)} %collective-permute-done.4), channel_id=1, source_target_pairs={{0,64},{8,72},{16,80},{24,88},{32,96},{40,104},{48,112},{56,120},{... | collective-permute-start | bytes 393224 | tf_op jit(solution)/shard_map/ppermute | solution.py:9
  79.4 2.5 collective-permute-done.5
  81.9 10.9 %collective-permute-start.6 = (bf16[512,128]{1,0:T(8,128)(2,1)S(1)}, bf16[512,128]{1,0:T(8,128)(2,1)S(1)}, u32[]{:S(2)}, u32[]{:S(2)}) collective-permute-start(bf16[512,128]{1,0:T(8,128)(2,1)S(1)} %collective-permute-done.5), channel_id=1, source_target_pairs={{0,64},{8,72},{16,80},{24,88},{32,96},{40,104},{48,112},{56,120},{... | collective-permute-start | bytes 393224 | tf_op jit(solution)/shard_map/ppermute | solution.py:9
  92.9 2.5 collective-permute-done.6
  95.4 10.9 %collective-permute-start.7 = (bf16[512,128]{1,0:T(8,128)(2,1)S(1)}, bf16[512,128]{1,0:T(8,128)(2,1)S(1)}, u32[]{:S(2)}, u32[]{:S(2)}) collective-permute-start(bf16[512,128]{1,0:T(8,128)(2,1)S(1)} %collective-permute-done.6), channel_id=1, source_target_pairs={{0,64},{8,72},{16,80},{24,88},{32,96},{40,104},{48,112},{56,120},{... | collective-permute-start | bytes 393224 | tf_op jit(solution)/shard_map/ppermute | solution.py:9
  106.3 2.5 collective-permute-done.7
  108.8 10.9 %collective-permute-start.8 = (bf16[512,128]{1,0:T(8,128)(2,1)S(1)}, bf16[512,128]{1,0:T(8,128)(2,1)}, u32[]{:S(2)}, u32[]{:S(2)}) collective-permute-start(bf16[512,128]{1,0:T(8,128)(2,1)S(1)} %collective-permute-done.7), channel_id=1, source_target_pairs={{0,64},{8,72},{16,80},{24,88},{32,96},{40,104},{48,112},{56,120},{... | collective-permute-start | bytes 393224 | tf_op jit(solution)/shard_map/ppermute | solution.py:9
  119.9 2.4 collective-permute-done.8
  122.3 11.1 %collective-permute-start.9 = (bf16[512,128]{1,0:T(8,128)(2,1)}, bf16[512,128]{1,0:T(8,128)(2,1)S(1)}, u32[]{:S(2)}, u32[]{:S(2)}) collective-permute-start(bf16[512,128]{1,0:T(8,128)(2,1)} %collective-permute-done.8), channel_id=1, source_target_pairs={{0,64},{8,72},{16,80},{24,88},{32,96},{40,104},{48,112},{56,120},{... | collective-permute-start | bytes 393224 | tf_op jit(solution)/shard_map/ppermute | solution.py:9
  133.3 1.5 compare_reduce_fusion
  139.8 0.7 convert_element_type.42
  140.5 1.4 fusion.34
  142.0 3.4 %conditional.9 = (f32[512,128]{1,0:T(8,128)S(1)}) conditional(s32[]{:T(128)} %convert_element_type.39, f32[512,128]{1,0:T(8,128)S(1)} %get-tuple-element.353, (bf16[1,1,6,512,512]{4,3,2,1,0:T(8,128)(2,1)}, bf16[512,128]{1,0:T(8,128)(2,1)S(1)}, f32[512,128]{1,0:T(8,128)S(1)}, s32[]{:T(128)}, s32[]{:T(128)}, /*index=5*/s32[]{:T(128)}, ...), branch_computations={%region_12.13_spmd, %region_13.14_spmd.clone} | conditional | flops 67174400 | bytes 1179694 | solution.py:36
  144.1 1.3 convolution_add_fusion.1
  145.5 0.0 collective-permute-done.9
  145.6 105.5 %all-reduce.1 = bf16[512,128]{1,0:T(8,128)(2,1)S(1)} all-reduce(f32[512,128]{1,0:T(8,128)S(1)} %get-tuple-element.360), channel_id=1, replica_groups=mesh['blk'=64,'rep'=8] {'rep'}, use_global_device_ids=true, to_apply=%region_32.33 | all-reduce | flops 65536 | bytes 393216 | tf_op jit(solution)/shard_map/psum | solution.py:42
  251.0 0.0 copy-done
  251.1 0.7 fusion.27
  (12 shorter events, 0.1 us)
Async XLA Ops:
  0.0 251.0 %copy-start = (bf16[128,128]{1,0:T(8,128)(2,1)S(1)}, bf16[128,128]{1,0:T(8,128)(2,1)}, u32[]{:S(2)}) copy-start(bf16[128,128]{1,0:T(8,128)(2,1)} %param.24) | copy-start | bytes 98308
  0.0 8.7 %collective-permute-start = (bf16[512,128]{1,0:T(8,128)(2,1)}, bf16[512,128]{1,0:T(8,128)(2,1)S(1)}, u32[]{:S(2)}, u32[]{:S(2)}) collective-permute-start(bf16[512,128]{1,0:T(8,128)(2,1)} %param.21), channel_id=1, source_target_pairs={{0,8},{8,16},{16,24},{24,32},{32,40},{40,48},{48,56},{56,64},{64,7... | collective-permute-start | bytes 393224 | tf_op jit(solution)/shard_map/ppermute | solution.py:9
  9.7 9.0 %collective-permute-start.1 = (bf16[512,128]{1,0:T(8,128)(2,1)S(1)}, bf16[512,128]{1,0:T(8,128)(2,1)S(1)}, u32[]{:S(2)}, u32[]{:S(2)}) collective-permute-start(bf16[512,128]{1,0:T(8,128)(2,1)S(1)} %broadcast_select_fusion), channel_id=1, source_target_pairs={{0,16},{8,24},{16,32},{24,40},{32,48},{40,56},{48,64},{56,72},{64,... | collective-permute-start | bytes 393224 | tf_op jit(solution)/shard_map/ppermute | solution.py:9
  18.6 9.3 %collective-permute-start.2 = (bf16[512,128]{1,0:T(8,128)(2,1)S(1)}, bf16[512,128]{1,0:T(8,128)(2,1)S(1)}, u32[]{:S(2)}, u32[]{:S(2)}) collective-permute-start(bf16[512,128]{1,0:T(8,128)(2,1)S(1)} %broadcast_select_fusion.1), channel_id=1, source_target_pairs={{0,32},{8,40},{16,48},{24,56},{32,64},{40,72},{48,80},{56,88},{64,... | collective-permute-start | bytes 393224 | tf_op jit(solution)/shard_map/ppermute | solution.py:9
  27.9 27.0 %collective-permute-start.3 = (bf16[512,128]{1,0:T(8,128)(2,1)S(1)}, bf16[512,128]{1,0:T(8,128)(2,1)S(1)}, u32[]{:S(2)}, u32[]{:S(2)}) collective-permute-start(bf16[512,128]{1,0:T(8,128)(2,1)S(1)} %broadcast_select_fusion.2), channel_id=1, source_target_pairs={{0,64},{8,72},{16,80},{24,88},{32,96},{40,104},{48,112},{56,120},{... | collective-permute-start | bytes 393224 | tf_op jit(solution)/shard_map/ppermute | solution.py:9
  55.0 13.5 %collective-permute-start.4 = (bf16[512,128]{1,0:T(8,128)(2,1)S(1)}, bf16[512,128]{1,0:T(8,128)(2,1)S(1)}, u32[]{:S(2)}, u32[]{:S(2)}) collective-permute-start(bf16[512,128]{1,0:T(8,128)(2,1)S(1)} %collective-permute-done.3), channel_id=1, source_target_pairs={{0,64},{8,72},{16,80},{24,88},{32,96},{40,104},{48,112},{56,120},{... | collective-permute-start | bytes 393224 | tf_op jit(solution)/shard_map/ppermute | solution.py:9
  68.5 13.5 %collective-permute-start.5 = (bf16[512,128]{1,0:T(8,128)(2,1)S(1)}, bf16[512,128]{1,0:T(8,128)(2,1)S(1)}, u32[]{:S(2)}, u32[]{:S(2)}) collective-permute-start(bf16[512,128]{1,0:T(8,128)(2,1)S(1)} %collective-permute-done.4), channel_id=1, source_target_pairs={{0,64},{8,72},{16,80},{24,88},{32,96},{40,104},{48,112},{56,120},{... | collective-permute-start | bytes 393224 | tf_op jit(solution)/shard_map/ppermute | solution.py:9
  81.9 13.5 %collective-permute-start.6 = (bf16[512,128]{1,0:T(8,128)(2,1)S(1)}, bf16[512,128]{1,0:T(8,128)(2,1)S(1)}, u32[]{:S(2)}, u32[]{:S(2)}) collective-permute-start(bf16[512,128]{1,0:T(8,128)(2,1)S(1)} %collective-permute-done.5), channel_id=1, source_target_pairs={{0,64},{8,72},{16,80},{24,88},{32,96},{40,104},{48,112},{56,120},{... | collective-permute-start | bytes 393224 | tf_op jit(solution)/shard_map/ppermute | solution.py:9
  95.4 13.5 %collective-permute-start.7 = (bf16[512,128]{1,0:T(8,128)(2,1)S(1)}, bf16[512,128]{1,0:T(8,128)(2,1)S(1)}, u32[]{:S(2)}, u32[]{:S(2)}) collective-permute-start(bf16[512,128]{1,0:T(8,128)(2,1)S(1)} %collective-permute-done.6), channel_id=1, source_target_pairs={{0,64},{8,72},{16,80},{24,88},{32,96},{40,104},{48,112},{56,120},{... | collective-permute-start | bytes 393224 | tf_op jit(solution)/shard_map/ppermute | solution.py:9
  108.8 13.5 %collective-permute-start.8 = (bf16[512,128]{1,0:T(8,128)(2,1)S(1)}, bf16[512,128]{1,0:T(8,128)(2,1)}, u32[]{:S(2)}, u32[]{:S(2)}) collective-permute-start(bf16[512,128]{1,0:T(8,128)(2,1)S(1)} %collective-permute-done.7), channel_id=1, source_target_pairs={{0,64},{8,72},{16,80},{24,88},{32,96},{40,104},{48,112},{56,120},{... | collective-permute-start | bytes 393224 | tf_op jit(solution)/shard_map/ppermute | solution.py:9
  122.3 23.2 %collective-permute-start.9 = (bf16[512,128]{1,0:T(8,128)(2,1)}, bf16[512,128]{1,0:T(8,128)(2,1)S(1)}, u32[]{:S(2)}, u32[]{:S(2)}) collective-permute-start(bf16[512,128]{1,0:T(8,128)(2,1)} %collective-permute-done.8), channel_id=1, source_target_pairs={{0,64},{8,72},{16,80},{24,88},{32,96},{40,104},{48,112},{56,120},{... | collective-permute-start | bytes 393224 | tf_op jit(solution)/shard_map/ppermute | solution.py:9
where the time goes:
time: 253 us; the launch traced here: 252 us
  blocking collectives  105 us (42%)
  starting transfers between devices  96.2 us (38%)
  waiting for transfers between devices  36 us (14%)
  between operations  5.36 us (2%)
  other arithmetic  4.53 us (2%)
    psum x1, blocking collectives, local(): summed = lax.psum(running, 'rep')  105 us
    ppermute x10, starting transfers between devices, passed_along(): lax.ppermute(array, axis, [(i, (i + by) % peers) for i in range(peers)])  96.2 us
    ppermute x10, waiting for transfers between devices, passed_along(): lax.ppermute(array, axis, [(i, (i + by) % peers) for i in range(peers)])  36 us
  transfers between devices with their start and end apart: 10, of which 9 were waited for; matrix products, arithmetic and copies ran while one was open for 2% of the time, Pallas kernels for 0%

commit v1 on v0

v1 whole, which is shorter than its diff:
```python
import functools

import jax
import jax.numpy as jnp
from jax import lax
from jax.experimental import pallas as pl
from jax.experimental.pallas import tpu as pltpu
from jax.sharding import PartitionSpec as P

SIDE, RING, LINE = 4, 16, 8


def device(x, y, z, core):
    x, y, z = x % SIDE, y % SIDE, z % RING
    return ((z % LINE * SIDE + x) * 2 + core) * LINE + y * 2 + z // LINE


def members(diagonal, half, core):
    kind = (2 * diagonal + core - half) % LINE
    by_hops = (1, 0, 2, 3) if half == 1 and core == 0 else (2, 1, 3, 0)
    return kind, by_hops


@functools.cache
def plan():
    groups, wanted = [], {}
    for low in range(0, RING, 2):
        half = low // LINE
        for diagonal in range(SIDE):
            for core in range(2):
                kind, by_hops = members(diagonal, half, core)
                group = []
                for offset in range(-3, 5):
                    z, hops = (low, -offset) if offset <= 0 else (low + 1, offset - 1)
                    y = by_hops[hops]
                    member = device(diagonal + y, y, z, core)
                    group.append(member)
                    wanted.setdefault(((low + offset) % RING, kind), []).append((y, member))
                groups.append(group)
    pairs = []
    for (z, kind), receivers in wanted.items():
        free = set(range(SIDE))
        for exact in (True, False):
            for y, member in receivers:
                if exact and y in free:
                    pass
                elif not exact and member not in placed:
                    y = min(free, key=lambda other: min((other - y) % SIDE, (y - other) % SIDE))
                else:
                    continue
                if exact:
                    placed = {m for _, m in pairs}
                free.discard(y)
                pairs.append((device(kind // 2, y, z, kind % 2), member))
            placed = {m for _, m in pairs}
    return groups, pairs


def aggregate_kernel(slots, order, adjacency, blocks, out, total):
    total[...] = jnp.zeros_like(total)
    for slot in range(adjacency.shape[0]):

        @pl.when(slots[slot] >= 0)
        def _():
            total[...] += jnp.dot(
                adjacency[slot], blocks[order[slot]], preferred_element_type=jnp.float32
            )

    out[...] = total[...].astype(out.dtype)


def project_kernel(parts, weight, bias, out):
    hidden = jnp.sum(parts[...].astype(jnp.float32), axis=0).astype(jnp.bfloat16)
    result = jnp.dot(hidden, weight[...], preferred_element_type=jnp.float32)
    out[...] = jnp.maximum(result + bias[...].astype(jnp.float32), 0.0).astype(out.dtype)


def local(features, adjacency, tile_column, weight, out_bias):
    groups, pairs = plan()
    axes = ("blk", "rep")
    rows, width = features.shape
    tiles = adjacency.reshape(adjacency.shape[2:])
    columns = tile_column.reshape(-1)
    low = lax.axis_index("blk") // LINE & ~1
    order = (columns // LINE - low + 3) & (LINE - 1)

    first = lax.ppermute(features, axes, pairs)
    blocks = lax.all_to_all(
        jnp.broadcast_to(first[None], (LINE, rows, width)), axes, 0, 0, axis_index_groups=groups
    )
    vmem, smem = pl.BlockSpec(memory_space=pltpu.VMEM), pl.BlockSpec(memory_space=pltpu.SMEM)
    partial = pl.pallas_call(
        aggregate_kernel,
        out_shape=jax.ShapeDtypeStruct((rows, width), jnp.bfloat16),
        in_specs=[smem, smem, vmem, vmem],
        out_specs=vmem,
        scratch_shapes=[pltpu.VMEM((rows, width), jnp.float32)],
        compiler_params=pltpu.CompilerParams(vmem_limit_bytes=16 * 2**20),
    )(columns, order, tiles, blocks)
    replicas = lax.axis_size("rep")
    parts = lax.all_to_all(partial.reshape(replicas, rows // replicas, width), "rep", 0, 0)
    return pl.pallas_call(
        project_kernel,
        out_shape=jax.ShapeDtypeStruct((rows // replicas, width), jnp.bfloat16),
        in_specs=[vmem, vmem, vmem],
        out_specs=vmem,
    )(parts, weight, out_bias.reshape(1, width))


def solution(mesh):
    in_specs = (P("blk", None), P("blk", "rep", None, None, None), P("blk", "rep", None), P(), P())
    out_specs = P(("blk", "rep"), None)
    return jax.shard_map(local, mesh=mesh, in_specs=in_specs, out_specs=out_specs, check_vma=False)
```

time: 253 us -> 75.7 us (0.30)
  the two profiles are of different devices: /device:TPU:224 before, /device:TPU:34 now
where the time goes in v1:
time: 75.7 us; the launch traced here: 75.5 us
  blocking collectives  28.4 us (38%)
  waiting for transfers between devices  22.5 us (30%)
  starting transfers between devices  18.7 us (25%)
  local copies, waits for them, and re-layouts  2.99 us (4%)
  Pallas kernels  2.86 us (4%)
    all_to_all x1, blocking collectives, local(): lax.all_to_all(partial.reshape(replicas, rows // replicas, width), 'rep',...  28.4 us
    all_to_all x1, waiting for transfers between devices, local(): lax.all_to_all(jnp.broadcast_to(first[None], (LINE, rows, width)), axes,...  18.8 us
    all_to_all x1, starting transfers between devices, local(): lax.all_to_all(jnp.broadcast_to(first[None], (LINE, rows, width)), axes,...  10.9 us
    ppermute x1, starting transfers between devices, local(): first = lax.ppermute(features, axes, pairs)  7.86 us
    ppermute x1, waiting for transfers between devices, local(): first = lax.ppermute(features, axes, pairs)  3.7 us
    unnamed x4, local copies, waits for them, and re-layouts  1.89 us
    pallas_call x1, Pallas kernels, local(): pl.pallas_call(project_kernel, out_shape=jax.ShapeDtypeStruct((rows // re...  1.67 us
  transfers between devices with their start and end apart: 2, of which 2 were waited for; matrix products, arithmetic and copies ran while one was open for 0% of the time, Pallas kernels for 0%

profile of v1, /device:TPU:34, one launch (start us, length us, event | category | flops | bytes accessed | tf_op | source)
XLA Modules:
  0.0 75.5 jit_solution(9782797224472949924)
XLA Ops:
  0.0 0.0 copy-start.1
  0.0 7.9 %collective-permute-start = (bf16[512,128]{1,0:T(8,128)(2,1)}, bf16[512,128]{1,0:T(8,128)(2,1)S(1)}, u32[]{:S(2)}, u32[]{:S(2)}) collective-permute-start(bf16[512,128]{1,0:T(8,128)(2,1)} %param.5), channel_id=1, source_target_pairs={{321,0},{327,255},{325,365},{323,411},{391,54},{385,201},{387,347}... | collective-permute-start | bytes 393224 | tf_op jit(solution)/shard_map/ppermute | solution.py:87
  7.9 3.7 %collective-permute-done = bf16[512,128]{1,0:T(8,128)(2,1)S(1)} collective-permute-done((bf16[512,128]{1,0:T(8,128)(2,1)}, bf16[512,128]{1,0:T(8,128)(2,1)S(1)}, u32[]{:S(2)}, u32[]{:S(2)}) %collective-permute-start) | collective-permute-done | bytes 131104 | tf_op jit(solution)/shard_map/ppermute | solution.py:87
  11.6 1.1 %broadcast_in_dim.2 = bf16[8,512,128]{2,1,0:T(8,128)(2,1)} broadcast(bf16[512,128]{1,0:T(8,128)(2,1)S(1)} %collective-permute-done), dimensions={1,2} | broadcast | bytes 1179648 | tf_op jit(solution)/shard_map/broadcast_in_dim | solution.py:89
  12.7 10.9 %all-to-all-start = ((bf16[8,512,128]{2,1,0:T(8,128)(2,1)}), bf16[8,512,128]{2,1,0:T(8,128)(2,1)S(1)}, u32[]{:S(2)}, u32[]{:S(2)}) async-start(bf16[8,512,128]{2,1,0:T(8,128)(2,1)} %broadcast_in_dim.2), calls=%async_computation | async-start | bytes 2097152 | tf_op jit(solution)/shard_map/all_to_all | solution.py:88
  23.6 0.0 copy-done.1
  23.6 18.8 %all-to-all-done.blocks = bf16[8,512,128]{2,1,0:T(8,128)(2,1)S(1)} async-done(((bf16[8,512,128]{2,1,0:T(8,128)(2,1)}), bf16[8,512,128]{2,1,0:T(8,128)(2,1)S(1)}, u32[]{:S(2)}, u32[]{:S(2)}) %all-to-all-start) | async-done | bytes 1048608 | tf_op jit(solution)/shard_map/all_to_all | solution.py:88
  42.3 0.0 copy-start
  42.3 1.9 %copy-done = bf16[1,1,6,512,512]{4,3,2,1,0:T(8,128)(2,1)S(1)} copy-done((bf16[1,1,6,512,512]{4,3,2,1,0:T(8,128)(2,1)S(1)}, bf16[1,1,6,512,512]{4,3,2,1,0:T(8,128)(2,1)}, u32[]{:S(2)}) %copy-start) | copy-done | bytes 3145752
  44.2 1.2 %shard_map.55 = bf16[512,128]{1,0:T(8,128)(2,1)S(1)} custom-call(s32[6]{0:T(128)S(1)} %bitcast.7, s32[6]{0:T(128)S(1)} %add_and_fusion.order, bf16[6,512,512]{2,1,0:T(8,128)(2,1)S(1)} %bitcast.5, bf16[8,512,128]{2,1,0:T(8,128)(2,1)S(1)} %all-to-all-done.blocks), custom_call_target="tpu_custom_call" | custom-call | tf_op jit(solution)/shard_map/pallas_call | solution.py:92
  45.4 28.4 %all_to_all.10.parts = bf16[8,64,128]{2,1,0:T(8,128)(2,1)} all-to-all(bf16[8,64,128]{2,1,0:T(8,128)(2,1)S(1)} %bitcast.6), channel_id=1, replica_groups=mesh['blk'=64,'rep'=8] {'rep'}, dimensions={0} | all-to-all | bytes 262144 | tf_op jit(solution)/shard_map/all_to_all | solution.py:101
  73.8 1.7 %shard_map.56 = bf16[64,128]{1,0:T(8,128)(2,1)} custom-call(bf16[8,64,128]{2,1,0:T(8,128)(2,1)} %all_to_all.10.parts, bf16[128,128]{1,0:T(8,128)(2,1)} %weight.1, bf16[1,128]{1,0:T(2,128)(2,1)} %bitcast.8), custom_call_target="tpu_custom_call" | custom-call | tf_op jit(solution)/shard_map/pallas_call | solution.py:102
  (1 shorter events, 0.0 us)
Async XLA Ops:
  0.0 23.6 %copy-start.1 = (s32[1,1,6]{2,1,0:T(1,128)S(1)}, s32[1,1,6]{2,1,0:T(1,128)}, u32[]{:S(2)}) copy-start(s32[1,1,6]{2,1,0:T(1,128)} %param.7) | copy-start | bytes 76
  0.0 11.6 %collective-permute-start = (bf16[512,128]{1,0:T(8,128)(2,1)}, bf16[512,128]{1,0:T(8,128)(2,1)S(1)}, u32[]{:S(2)}, u32[]{:S(2)}) collective-permute-start(bf16[512,128]{1,0:T(8,128)(2,1)} %param.5), channel_id=1, source_target_pairs={{321,0},{327,255},{325,365},{323,411},{391,54},{385,201},{387,347}... | collective-permute-start | bytes 393224 | tf_op jit(solution)/shard_map/ppermute | solution.py:87
  12.7 29.7 %all-to-all-start = ((bf16[8,512,128]{2,1,0:T(8,128)(2,1)}), bf16[8,512,128]{2,1,0:T(8,128)(2,1)S(1)}, u32[]{:S(2)}, u32[]{:S(2)}) async-start(bf16[8,512,128]{2,1,0:T(8,128)(2,1)} %broadcast_in_dim.2), calls=%async_computation | async-start | bytes 2097152 | tf_op jit(solution)/shard_map/all_to_all | solution.py:88
  42.3 1.9 %copy-start = (bf16[1,1,6,512,512]{4,3,2,1,0:T(8,128)(2,1)S(1)}, bf16[1,1,6,512,512]{4,3,2,1,0:T(8,128)(2,1)}, u32[]{:S(2)}) copy-start(bf16[1,1,6,512,512]{4,3,2,1,0:T(8,128)(2,1)} %param.6) | copy-start | bytes 9437188

commit v2 on v1

v2 whole, which is shorter than its diff:
```python
import functools
import itertools

import jax
import jax.numpy as jnp
from jax import lax
from jax.experimental import pallas as pl
from jax.experimental.pallas import tpu as pltpu
from jax.sharding import PartitionSpec as P

SIDE, RING, LINE = 4, 16, 8
BY_HOPS = (2, 1, 3, 0), (1, 0, 2, 3)
REDUCE_ORDER = 1, 3, 5, 7, 0, 2, 4, 6


def device(x, y, z, core):
    x, y, z = x % SIDE, y % SIDE, z % RING
    return ((z % LINE * SIDE + x) * 2 + core) * LINE + y * 2 + z // LINE


def apart(one, other, size):
    return min((one - other) % size, (other - one) % size)


@functools.cache
def plan():
    groups, receivers = [], {}
    for low in range(0, RING, 2):
        half = low // LINE
        for diagonal, core in itertools.product(range(SIDE), range(2)):
            kind = (2 * diagonal + core - half) % LINE
            by_hops = BY_HOPS[half == 1 and core == 0]
            group = []
            for later, at in itertools.product(range(2), range(SIDE)):
                hops = (at - 1) % SIDE
                y = by_hops[hops]
                place = ((diagonal + y) % SIDE, y, low + later, core)
                group.append(device(*place))
                key = (low + later + (hops if later else -hops)) % RING, kind
                receivers.setdefault(key, []).append(place)
            groups.append(group)
    pairs = []
    for (z, kind), places in receivers.items():

        def cost(rows):
            hops = [
                apart(kind // 2, place[0], SIDE) + apart(row, place[1], SIDE) + apart(z, place[2], RING)
                for row, place in zip(rows, places)
            ]
            return max(hops), sum(hops)

        rows = min(itertools.permutations(range(SIDE)), key=cost)
        pairs += [
            (device(kind // 2, row, z, kind % 2), device(*place)) for row, place in zip(rows, places)
        ]
    return groups, pairs


def aggregate_kernel(columns, adjacency, blocks, out, total):
    low = lax.axis_index("blk") // LINE & ~1
    slots = range(adjacency.shape[0])
    total[...] = jnp.zeros_like(total)
    for slot in slots:

        @pl.when(columns[slot] >= 0)
        def _():
            ahead = (columns[slot] // LINE - low + 3) & (LINE - 1)
            hops = jnp.where(ahead > 3, ahead - 4, 3 - ahead)
            place = (ahead & 4) + ((hops + 1) & 3)
            total[...] += jnp.dot(adjacency[slot], blocks[place], preferred_element_type=jnp.float32)

    own = out.shape[1]
    for at, replica in enumerate(REDUCE_ORDER):
        out[at] = total[replica * own : (replica + 1) * own].astype(out.dtype)


def project_kernel(parts, weight, bias, out):
    hidden = jnp.sum(parts[...].astype(jnp.float32), axis=0).astype(jnp.bfloat16)
    result = jnp.dot(hidden, weight[...], preferred_element_type=jnp.float32)
    out[...] = jnp.maximum(result + bias[...].astype(jnp.float32), 0.0).astype(out.dtype)


def local(features, adjacency, tile_column, weight, out_bias):
    groups, pairs = plan()
    axes = ("blk", "rep")
    rows, width = features.shape
    replicas = lax.axis_size("rep")

    first = lax.ppermute(features, axes, pairs)
    blocks = lax.all_to_all(
        jnp.broadcast_to(first[None], (LINE, rows, width)), axes, 0, 0, axis_index_groups=groups
    )
    vmem, smem = pl.BlockSpec(memory_space=pltpu.VMEM), pl.BlockSpec(memory_space=pltpu.SMEM)
    partial = pl.pallas_call(
        aggregate_kernel,
        out_shape=jax.ShapeDtypeStruct((replicas, rows // replicas, width), jnp.bfloat16),
        in_specs=[smem, vmem, vmem],
        out_specs=vmem,
        scratch_shapes=[
            pltpu.VMEM((rows, width), jnp.float32),
        ],
        compiler_params=pltpu.CompilerParams(vmem_limit_bytes=8 * 2**20),
    )(tile_column.reshape(-1), adjacency.reshape(adjacency.shape[2:]), blocks)
    parts = lax.all_to_all(partial, "rep", 0, 0, axis_index_groups=[list(REDUCE_ORDER)])
    return pl.pallas_call(
        project_kernel,
        out_shape=jax.ShapeDtypeStruct((rows // replicas, width), jnp.bfloat16),
        in_specs=[vmem, vmem, vmem],
        out_specs=vmem,
        compiler_params=pltpu.CompilerParams(vmem_limit_bytes=4 * 2**20),
    )(parts, weight, out_bias.reshape(1, width))


def solution(mesh):
    in_specs = (P("blk", None), P("blk", "rep", None, None, None), P("blk", "rep", None), P(), P())
    out_specs = P(("blk", "rep"), None)
    return jax.shard_map(local, mesh=mesh, in_specs=in_specs, out_specs=out_specs, check_vma=False)
```

time: 75.7 us -> 62.8 us (0.83)
  the two profiles are of different devices: /device:TPU:34 before, /device:TPU:39 now
where the time goes in v2:
time: 62.8 us; the launch traced here: 62.6 us
  blocking collectives  49 us (78%)
  starting transfers between devices  7.71 us (12%)
  waiting for transfers between devices  3.42 us (5%)
  Pallas kernels  2.26 us (4%)
    all_to_all x1, blocking collectives, local(): lax.all_to_all(jnp.broadcast_to(first[None], (LINE, rows, width)), axes,...  27.5 us
    all_to_all x1, blocking collectives, local(): lax.all_to_all(partial, 'rep', 0, 0, axis_index_groups=[list(REDUCE_ORDER)])  21.5 us
    ppermute x1, starting transfers between devices, local(): first = lax.ppermute(features, axes, pairs)  7.71 us
    ppermute x1, waiting for transfers between devices, local(): first = lax.ppermute(features, axes, pairs)  3.42 us
    pallas_call x1, Pallas kernels, local(): pl.pallas_call(aggregate_kernel, out_shape=jax.ShapeDtypeStruct((replicas...  1.51 us
  transfers between devices with their start and end apart: 1, of which 1 were waited for; matrix products, arithmetic and copies ran while one was open for 0% of the time, Pallas kernels for 0%

profile of v2, /device:TPU:39, one launch (start us, length us, event | category | flops | bytes accessed | tf_op | source)
XLA Modules:
  0.0 62.6 jit_solution(12748113051388925127)
XLA Ops:
  0.0 0.0 copy-start.2
  0.0 0.0 copy-start
  0.0 7.7 %collective-permute-start = (bf16[512,128]{1,0:T(8,128)(2,1)}, bf16[512,128]{1,0:T(8,128)(2,1)S(1)}, u32[]{:S(2)}, u32[]{:S(2)}) collective-permute-start(bf16[512,128]{1,0:T(8,128)(2,1)} %param.5), channel_id=1, source_target_pairs={{321,0},{327,255},{325,365},{323,411},{4,36},{6,182},{0,329},{2,47... | collective-permute-start | bytes 393224 | tf_op jit(solution)/shard_map/ppermute | solution.py:89
  7.7 3.4 %collective-permute-done = bf16[512,128]{1,0:T(8,128)(2,1)S(1)} collective-permute-done((bf16[512,128]{1,0:T(8,128)(2,1)}, bf16[512,128]{1,0:T(8,128)(2,1)S(1)}, u32[]{:S(2)}, u32[]{:S(2)}) %collective-permute-start) | collective-permute-done | bytes 131104 | tf_op jit(solution)/shard_map/ppermute | solution.py:89
  11.1 0.1 broadcast_in_dim.2
  11.3 0.0 copy-start.1
  11.3 0.0 copy-start.3
  11.3 27.5 %all_to_all.10.blocks = bf16[8,512,128]{2,1,0:T(8,128)(2,1)S(1)} all-to-all(bf16[8,512,128]{2,1,0:T(8,128)(2,1)S(1)} %broadcast_in_dim.2), channel_id=1, replica_groups={{0,36,18,54,64,100,82,118},{8,44,26,62,72,108,90,126},{16,52,34,6,80,11..., dimensions={0} | all-to-all | bytes 2097152 | tf_op jit(solution)/shard_map/all_to_all | solution.py:90
  38.8 0.0 copy-done.2
  38.8 0.0 copy-done
  38.8 1.5 %shard_map.55 = bf16[8,64,128]{2,1,0:T(8,128)(2,1)S(1)} custom-call(s32[6]{0:T(128)S(1)} %bitcast.4, bf16[6,512,512]{2,1,0:T(8,128)(2,1)S(1)} %bitcast.3, bf16[8,512,128]{2,1,0:T(8,128)(2,1)S(1)} %all_to_all.10.blocks), custom_call_target="tpu_custom_call" | custom-call | tf_op jit(solution)/shard_map/pallas_call | solution.py:94
  40.3 21.5 %all_to_all.11.parts = bf16[8,64,128]{2,1,0:T(8,128)(2,1)S(1)} all-to-all(bf16[8,64,128]{2,1,0:T(8,128)(2,1)S(1)} %shard_map.55), channel_id=1, replica_groups={{1,3,5,7,0,2,4,6},{9,11,13,15,8,10,12,14},{17,19,21,23,16,18,20,22},{25..., dimensions={0} | all-to-all | bytes 262144 | tf_op jit(solution)/shard_map/all_to_all | solution.py:104
  61.9 0.0 copy-done.1
  61.9 0.0 copy-done.3
  61.9 0.8 %shard_map.56 = bf16[64,128]{1,0:T(8,128)(2,1)} custom-call(bf16[8,64,128]{2,1,0:T(8,128)(2,1)S(1)} %all_to_all.11.parts, bf16[128,128]{1,0:T(8,128)(2,1)S(1)} %copy-done.1, bf16[1,128]{1,0:T(2,128)(2,1)S(1)} %bitcast.5), custom_call_target="tpu_custom_call" | custom-call | tf_op jit(solution)/shard_map/pallas_call | solution.py:105
Async XLA Ops:
  0.0 38.8 %copy-start.2 = (s32[1,1,6]{2,1,0:T(1,128)S(1)}, s32[1,1,6]{2,1,0:T(1,128)}, u32[]{:S(2)}) copy-start(s32[1,1,6]{2,1,0:T(1,128)} %param.7) | copy-start | bytes 76
  0.0 38.8 %copy-start = (bf16[1,1,6,512,512]{4,3,2,1,0:T(8,128)(2,1)S(1)}, bf16[1,1,6,512,512]{4,3,2,1,0:T(8,128)(2,1)}, u32[]{:S(2)}) copy-start(bf16[1,1,6,512,512]{4,3,2,1,0:T(8,128)(2,1)} %param.6) | copy-start | bytes 9437188
  0.0 11.1 %collective-permute-start = (bf16[512,128]{1,0:T(8,128)(2,1)}, bf16[512,128]{1,0:T(8,128)(2,1)S(1)}, u32[]{:S(2)}, u32[]{:S(2)}) collective-permute-start(bf16[512,128]{1,0:T(8,128)(2,1)} %param.5), channel_id=1, source_target_pairs={{321,0},{327,255},{325,365},{323,411},{4,36},{6,182},{0,329},{2,47... | collective-permute-start | bytes 393224 | tf_op jit(solution)/shard_map/ppermute | solution.py:89
  11.3 50.6 %copy-start.1 = (bf16[128,128]{1,0:T(8,128)(2,1)S(1)}, bf16[128,128]{1,0:T(8,128)(2,1)}, u32[]{:S(2)}) copy-start(bf16[128,128]{1,0:T(8,128)(2,1)} %weight.1) | copy-start | bytes 98308
  11.3 50.6 %copy-start.3 = (bf16[128]{0:T(256)(128)(2,1)S(1)}, bf16[128]{0:T(256)(128)(2,1)}, u32[]{:S(2)}) copy-start(bf16[128]{0:T(256)(128)(2,1)} %param.9) | copy-start | bytes 772

commit v3 on v2

v3 whole, which is shorter than its diff:
```python
import functools
import itertools

import jax
import jax.numpy as jnp
from jax import lax
from jax.experimental import pallas as pl
from jax.experimental.pallas import tpu as pltpu
from jax.sharding import PartitionSpec as P

SIDE, RING, LINE = 4, 16, 8
REDUCE_ORDER = 1, 3, 5, 7, 0, 2, 4, 6


def device(x, y, z, core):
    x, y, z = x % SIDE, y % SIDE, z % RING
    return ((z % LINE * SIDE + x) * 2 + core) * LINE + y * 2 + z // LINE


def user(kind, y, z):
    half = z % RING // LINE
    core = (kind + half) % 2
    return ((kind - core + half) // 2 + y) % SIDE, y, z % RING, core


def apart(one, other, size):
    return min((one - other) % size, (other - one) % size)


@functools.cache
def plan():
    groups, receivers = [], ({}, {})
    for kind in range(LINE):
        even = 1 - kind % 2
        for low, first in itertools.product(range(even, RING, 2), (even, even + 2)):
            group = []
            for z in (low, low + 1):
                pair = [user(kind, (first + i) % SIDE, z) for i in range(2)]
                group += sorted(pair, key=lambda place: apart(place[0], kind // 2, SIDE))
            groups.append([device(*place) for place in group])
            for later, at in itertools.product(range(2), range(SIDE)):
                hops = SIDE - 1 - at
                key = (low + later + (hops if later else -hops)) % RING, kind
                receivers[at % 2].setdefault(key, []).append(group[2 * later + at // 2])
    permutes = []
    for wanted in receivers:
        pairs = []
        for (z, kind), places in wanted.items():

            def cost(rows):
                hops = [
                    apart(kind // 2, place[0], SIDE) + apart(row, place[1], SIDE) + apart(z, place[2], RING)
                    for row, place in zip(rows, places)
                ]
                return max(hops), sum(hops)

            rows = min(itertools.permutations(range(SIDE)), key=cost)
            pairs += [
                (device(kind // 2, row, z, kind % 2), device(*place)) for row, place in zip(rows, places)
            ]
        permutes.append(pairs)
    return groups, permutes


def aggregate_kernel(columns, adjacency, blocks, out):
    blk, rep = lax.axis_index("blk"), lax.axis_index("rep")
    low = blk // LINE - ((blk // LINE ^ blk ^ rep ^ 1) & 1)
    slots = range(adjacency.shape[0])
    total = None
    for slot in slots:
        ahead = (columns[slot] // LINE - low + 3) & (LINE - 1)
        block = blocks[jnp.where(ahead > 3, ahead ^ 3, ahead)]
        block = jnp.where(columns[slot] >= 0, block, jnp.zeros_like(block))
        product = jnp.dot(adjacency[slot], block, preferred_element_type=jnp.float32)
        total = product if total is None else total + product

    own = out.shape[1]
    for at, replica in enumerate(REDUCE_ORDER):
        out[at] = total[replica * own : (replica + 1) * own].astype(out.dtype)


def project_kernel(parts, weight, bias, out):
    hidden = jnp.sum(parts[...].astype(jnp.float32), axis=0).astype(jnp.bfloat16)
    result = jnp.dot(hidden, weight[...], preferred_element_type=jnp.float32)
    out[...] = jnp.maximum(result + bias[...].astype(jnp.float32), 0.0).astype(out.dtype)


def local(features, adjacency, tile_column, weight, out_bias):
    groups, permutes = plan()
    axes = ("blk", "rep")
    rows, width = features.shape
    replicas = lax.axis_size("rep")

    held = jnp.stack([lax.ppermute(features, axes, pairs) for pairs in permutes])
    blocks = lax.all_to_all(
        jnp.broadcast_to(held[None], (len(groups[0]),) + held.shape), axes, 0, 0, axis_index_groups=groups
    ).reshape(LINE, rows, width)
    vmem, smem = pl.BlockSpec(memory_space=pltpu.VMEM), pl.BlockSpec(memory_space=pltpu.SMEM)
    partial = pl.pallas_call(
        aggregate_kernel,
        out_shape=jax.ShapeDtypeStruct((replicas, rows // replicas, width), jnp.bfloat16),
        in_specs=[smem, vmem, vmem],
        out_specs=vmem,
        compiler_params=pltpu.CompilerParams(vmem_limit_bytes=8 * 2**20),
    )(tile_column.reshape(-1), adjacency.reshape(adjacency.shape[2:]), blocks)
    parts = lax.all_to_all(partial, "rep", 0, 0, axis_index_groups=[list(REDUCE_ORDER)])
    return pl.pallas_call(
        project_kernel,
        out_shape=jax.ShapeDtypeStruct((rows // replicas, width), jnp.bfloat16),
        in_specs=[vmem, vmem, vmem],
        out_specs=vmem,
        compiler_params=pltpu.CompilerParams(vmem_limit_bytes=4 * 2**20),
    )(parts, weight, out_bias.reshape(1, width))


def solution(mesh):
    in_specs = (P("blk", None), P("blk", "rep", None, None, None), P("blk", "rep", None), P(), P())
    out_specs = P(("blk", "rep"), None)
    return jax.shard_map(local, mesh=mesh, in_specs=in_specs, out_specs=out_specs, check_vma=False)
```

time: 62.8 us -> 58.3 us (0.928)
  the two profiles are of different devices: /device:TPU:39 before, /device:TPU:448 now
where the time goes in v3:
time: 58.3 us; the launch traced here: 58 us
  blocking collectives  40.8 us (70%)
  waiting for transfers between devices  9.69 us (17%)
  starting transfers between devices  4.97 us (9%)
  Pallas kernels  2.31 us (4%)
    all_to_all x1, blocking collectives, local(): lax.all_to_all(partial, 'rep', 0, 0, axis_index_groups=[list(REDUCE_ORDER)])  27.6 us
    all_to_all x1, blocking collectives, local(): lax.all_to_all(jnp.broadcast_to(held[None], (len(groups[0]),) + held.shap...  13.3 us
    ppermute x2, waiting for transfers between devices, local(): lax.ppermute(features, axes, pairs)  9.69 us
    ppermute x2, starting transfers between devices, local(): lax.ppermute(features, axes, pairs)  4.97 us
    pallas_call x1, Pallas kernels, local(): pl.pallas_call(aggregate_kernel, out_shape=jax.ShapeDtypeStruct((replicas...  1.56 us
  transfers between devices with their start and end apart: 2, of which 2 were waited for; matrix products, arithmetic and copies ran while one was open for 0% of the time, Pallas kernels for 0%

profile of v3, /device:TPU:448, one launch (start us, length us, event | category | flops | bytes accessed | tf_op | source)
XLA Modules:
  0.0 58.0 jit_solution(3444993509050260861)
XLA Ops:
  0.0 0.0 copy-start.2
  0.0 0.0 copy-start
  0.0 3.0 %collective-permute-start.1 = (bf16[512,128]{1,0:T(8,128)(2,1)}, bf16[512,128]{1,0:T(8,128)(2,1)S(1)}, u32[]{:S(2)}, u32[]{:S(2)}) collective-permute-start(bf16[512,128]{1,0:T(8,128)(2,1)} %param.5), channel_id=1, source_target_pairs={{451,82},{449,64},{453,493},{455,511},{68,100},{70,118},{66,210},{... | collective-permute-start | bytes 393224 | tf_op jit(solution)/shard_map/ppermute | solution.py:94
  3.1 1.9 %collective-permute-start = (bf16[512,128]{1,0:T(8,128)(2,1)}, bf16[512,128]{1,0:T(8,128)(2,1)S(1)}, u32[]{:S(2)}, u32[]{:S(2)}) collective-permute-start(bf16[512,128]{1,0:T(8,128)(2,1)} %param.5), channel_id=1, source_target_pairs={{387,82},{385,64},{389,493},{391,511},{4,100},{6,118},{2,210},{0,1... | collective-permute-start | bytes 393224 | tf_op jit(solution)/shard_map/ppermute | solution.py:94
  5.0 4.9 %collective-permute-done.1 = bf16[512,128]{1,0:T(8,128)(2,1)S(1)} collective-permute-done((bf16[512,128]{1,0:T(8,128)(2,1)}, bf16[512,128]{1,0:T(8,128)(2,1)S(1)}, u32[]{:S(2)}, u32[]{:S(2)}) %collective-permute-start.1) | collective-permute-done | bytes 131104 | tf_op jit(solution)/shard_map/ppermute | solution.py:94
  9.9 4.8 %collective-permute-done = bf16[512,128]{1,0:T(8,128)(2,1)S(1)} collective-permute-done((bf16[512,128]{1,0:T(8,128)(2,1)}, bf16[512,128]{1,0:T(8,128)(2,1)S(1)}, u32[]{:S(2)}, u32[]{:S(2)}) %collective-permute-start) | collective-permute-done | bytes 131104 | tf_op jit(solution)/shard_map/ppermute | solution.py:94
  14.7 0.1 broadcast_in_dim.2
  14.9 0.0 copy-start.1
  14.9 0.0 copy-start.3
  14.9 13.3 %all_to_all.10 = bf16[4,2,512,128]{3,2,1,0:T(8,128)(2,1)S(1)} all-to-all(bf16[4,2,512,128]{3,2,1,0:T(8,128)(2,1)S(1)} %broadcast_in_dim.2), channel_id=1, replica_groups={{82,100,146,164},{64,118,128,182},{210,228,274,292},{192,246,256,310},{..., dimensions={0} | all-to-all | bytes 2097152 | tf_op jit(solution)/shard_map/all_to_all | solution.py:95
  28.1 0.0 copy-done.2
  28.1 0.0 copy-done
  28.1 1.6 %shard_map.55 = bf16[8,64,128]{2,1,0:T(8,128)(2,1)S(1)} custom-call(s32[6]{0:T(128)S(1)} %bitcast.8, bf16[6,512,512]{2,1,0:T(8,128)(2,1)S(1)} %bitcast.7, bf16[8,512,128]{2,1,0:T(8,128)(2,1)S(1)} %bitcast.6), custom_call_target="tpu_custom_call" | custom-call | tf_op jit(solution)/shard_map/pallas_call | solution.py:99
  29.7 27.6 %all_to_all.11.parts = bf16[8,64,128]{2,1,0:T(8,128)(2,1)S(1)} all-to-all(bf16[8,64,128]{2,1,0:T(8,128)(2,1)S(1)} %shard_map.55), channel_id=1, replica_groups={{1,3,5,7,0,2,4,6},{9,11,13,15,8,10,12,14},{17,19,21,23,16,18,20,22},{25..., dimensions={0} | all-to-all | bytes 262144 | tf_op jit(solution)/shard_map/all_to_all | solution.py:106
  57.3 0.0 copy-done.1
  57.3 0.0 copy-done.3
  57.3 0.8 %shard_map.56 = bf16[64,128]{1,0:T(8,128)(2,1)} custom-call(bf16[8,64,128]{2,1,0:T(8,128)(2,1)S(1)} %all_to_all.11.parts, bf16[128,128]{1,0:T(8,128)(2,1)S(1)} %copy-done.1, bf16[1,128]{1,0:T(2,128)(2,1)S(1)} %bitcast.9), custom_call_target="tpu_custom_call" | custom-call | tf_op jit(solution)/shard_map/pallas_call | solution.py:107
  (1 shorter events, 0.0 us)
Async XLA Ops:
  0.0 28.1 %copy-start.2 = (s32[1,1,6]{2,1,0:T(1,128)S(1)}, s32[1,1,6]{2,1,0:T(1,128)}, u32[]{:S(2)}) copy-start(s32[1,1,6]{2,1,0:T(1,128)} %param.7) | copy-start | bytes 76
  0.0 28.1 %copy-start = (bf16[1,1,6,512,512]{4,3,2,1,0:T(8,128)(2,1)S(1)}, bf16[1,1,6,512,512]{4,3,2,1,0:T(8,128)(2,1)}, u32[]{:S(2)}) copy-start(bf16[1,1,6,512,512]{4,3,2,1,0:T(8,128)(2,1)} %param.6) | copy-start | bytes 9437188
  0.0 9.9 %collective-permute-start.1 = (bf16[512,128]{1,0:T(8,128)(2,1)}, bf16[512,128]{1,0:T(8,128)(2,1)S(1)}, u32[]{:S(2)}, u32[]{:S(2)}) collective-permute-start(bf16[512,128]{1,0:T(8,128)(2,1)} %param.5), channel_id=1, source_target_pairs={{451,82},{449,64},{453,493},{455,511},{68,100},{70,118},{66,210},{... | collective-permute-start | bytes 393224 | tf_op jit(solution)/shard_map/ppermute | solution.py:94
  3.1 11.6 %collective-permute-start = (bf16[512,128]{1,0:T(8,128)(2,1)}, bf16[512,128]{1,0:T(8,128)(2,1)S(1)}, u32[]{:S(2)}, u32[]{:S(2)}) collective-permute-start(bf16[512,128]{1,0:T(8,128)(2,1)} %param.5), channel_id=1, source_target_pairs={{387,82},{385,64},{389,493},{391,511},{4,100},{6,118},{2,210},{0,1... | collective-permute-start | bytes 393224 | tf_op jit(solution)/shard_map/ppermute | solution.py:94
  14.9 42.4 %copy-start.1 = (bf16[128,128]{1,0:T(8,128)(2,1)S(1)}, bf16[128,128]{1,0:T(8,128)(2,1)}, u32[]{:S(2)}) copy-start(bf16[128,128]{1,0:T(8,128)(2,1)} %weight.1) | copy-start | bytes 98308
  14.9 42.4 %copy-start.3 = (bf16[128]{0:T(256)(128)(2,1)S(1)}, bf16[128]{0:T(256)(128)(2,1)}, u32[]{:S(2)}) copy-start(bf16[128]{0:T(256)(128)(2,1)} %param.9) | copy-start | bytes 772

commit v4 on v3

--- a/solution.py
+++ b/solution.py
@@ -9,7 +9,7 @@
 from jax.sharding import PartitionSpec as P
 
 SIDE, RING, LINE = 4, 16, 8
-REDUCE_ORDER = 1, 3, 5, 7, 0, 2, 4, 6
+REDUCE_ORDER = 1, 0, 3, 2, 5, 4, 7, 6
 
 
 def device(x, y, z, core):

time: 58.3 us -> 58.4 us (level)
  no operation moved by 1% of the time
where the time goes in v4:
time: 58.4 us; the launch traced here: 58.2 us
  blocking collectives  41 us (70%)
  waiting for transfers between devices  9.69 us (17%)
  starting transfers between devices  4.97 us (9%)
  Pallas kernels  2.31 us (4%)
    all_to_all x1, blocking collectives, local(): lax.all_to_all(partial, 'rep', 0, 0, axis_index_groups=[list(REDUCE_ORDER)])  27.7 us
    all_to_all x1, blocking collectives, local(): lax.all_to_all(jnp.broadcast_to(held[None], (len(groups[0]),) + held.shap...  13.3 us
    ppermute x2, waiting for transfers between devices, local(): lax.ppermute(features, axes, pairs)  9.69 us
    ppermute x2, starting transfers between devices, local(): lax.ppermute(features, axes, pairs)  4.97 us
    pallas_call x1, Pallas kernels, local(): pl.pallas_call(aggregate_kernel, out_shape=jax.ShapeDtypeStruct((replicas...  1.56 us
  transfers between devices with their start and end apart: 2, of which 2 were waited for; matrix products, arithmetic and copies ran while one was open for 0% of the time, Pallas kernels for 0%

profile of v4, /device:TPU:448, one launch (start us, length us, event | category | flops | bytes accessed | tf_op | source)
XLA Modules:
  0.0 58.2 jit_solution(4906425077140520906)
XLA Ops:
  0.0 0.0 copy-start.2
  0.0 0.0 copy-start
  0.0 3.0 %collective-permute-start.1 = (bf16[512,128]{1,0:T(8,128)(2,1)}, bf16[512,128]{1,0:T(8,128)(2,1)S(1)}, u32[]{:S(2)}, u32[]{:S(2)}) collective-permute-start(bf16[512,128]{1,0:T(8,128)(2,1)} %param.5), channel_id=1, source_target_pairs={{451,82},{449,64},{453,493},{455,511},{68,100},{70,118},{66,210},{... | collective-permute-start | bytes 393224 | tf_op jit(solution)/shard_map/ppermute | solution.py:94
  3.1 1.9 %collective-permute-start = (bf16[512,128]{1,0:T(8,128)(2,1)}, bf16[512,128]{1,0:T(8,128)(2,1)S(1)}, u32[]{:S(2)}, u32[]{:S(2)}) collective-permute-start(bf16[512,128]{1,0:T(8,128)(2,1)} %param.5), channel_id=1, source_target_pairs={{387,82},{385,64},{389,493},{391,511},{4,100},{6,118},{2,210},{0,1... | collective-permute-start | bytes 393224 | tf_op jit(solution)/shard_map/ppermute | solution.py:94
  5.0 4.9 %collective-permute-done.1 = bf16[512,128]{1,0:T(8,128)(2,1)S(1)} collective-permute-done((bf16[512,128]{1,0:T(8,128)(2,1)}, bf16[512,128]{1,0:T(8,128)(2,1)S(1)}, u32[]{:S(2)}, u32[]{:S(2)}) %collective-permute-start.1) | collective-permute-done | bytes 131104 | tf_op jit(solution)/shard_map/ppermute | solution.py:94
  9.9 4.8 %collective-permute-done = bf16[512,128]{1,0:T(8,128)(2,1)S(1)} collective-permute-done((bf16[512,128]{1,0:T(8,128)(2,1)}, bf16[512,128]{1,0:T(8,128)(2,1)S(1)}, u32[]{:S(2)}, u32[]{:S(2)}) %collective-permute-start) | collective-permute-done | bytes 131104 | tf_op jit(solution)/shard_map/ppermute | solution.py:94
  14.7 0.1 broadcast_in_dim.2
  14.9 0.0 copy-start.1
  14.9 0.0 copy-start.3
  14.9 13.3 %all_to_all.10 = bf16[4,2,512,128]{3,2,1,0:T(8,128)(2,1)S(1)} all-to-all(bf16[4,2,512,128]{3,2,1,0:T(8,128)(2,1)S(1)} %broadcast_in_dim.2), channel_id=1, replica_groups={{82,100,146,164},{64,118,128,182},{210,228,274,292},{192,246,256,310},{..., dimensions={0} | all-to-all | bytes 2097152 | tf_op jit(solution)/shard_map/all_to_all | solution.py:95
  28.1 0.0 copy-done.2
  28.1 0.0 copy-done
  28.1 1.6 %shard_map.55 = bf16[8,64,128]{2,1,0:T(8,128)(2,1)S(1)} custom-call(s32[6]{0:T(128)S(1)} %bitcast.8, bf16[6,512,512]{2,1,0:T(8,128)(2,1)S(1)} %bitcast.7, bf16[8,512,128]{2,1,0:T(8,128)(2,1)S(1)} %bitcast.6), custom_call_target="tpu_custom_call" | custom-call | tf_op jit(solution)/shard_map/pallas_call | solution.py:99
  29.7 27.7 %all_to_all.11.parts = bf16[8,64,128]{2,1,0:T(8,128)(2,1)S(1)} all-to-all(bf16[8,64,128]{2,1,0:T(8,128)(2,1)S(1)} %shard_map.55), channel_id=1, replica_groups={{1,0,3,2,5,4,7,6},{9,8,11,10,13,12,15,14},{17,16,19,18,21,20,23,22},{25..., dimensions={0} | all-to-all | bytes 262144 | tf_op jit(solution)/shard_map/all_to_all | solution.py:106
  57.4 0.0 copy-done.1
  57.4 0.0 copy-done.3
  57.4 0.8 %shard_map.56 = bf16[64,128]{1,0:T(8,128)(2,1)} custom-call(bf16[8,64,128]{2,1,0:T(8,128)(2,1)S(1)} %all_to_all.11.parts, bf16[128,128]{1,0:T(8,128)(2,1)S(1)} %copy-done.1, bf16[1,128]{1,0:T(2,128)(2,1)S(1)} %bitcast.9), custom_call_target="tpu_custom_call" | custom-call | tf_op jit(solution)/shard_map/pallas_call | solution.py:107
  (1 shorter events, 0.0 us)
Async XLA Ops:
  0.0 28.1 %copy-start.2 = (s32[1,1,6]{2,1,0:T(1,128)S(1)}, s32[1,1,6]{2,1,0:T(1,128)}, u32[]{:S(2)}) copy-start(s32[1,1,6]{2,1,0:T(1,128)} %param.7) | copy-start | bytes 76
  0.0 28.1 %copy-start = (bf16[1,1,6,512,512]{4,3,2,1,0:T(8,128)(2,1)S(1)}, bf16[1,1,6,512,512]{4,3,2,1,0:T(8,128)(2,1)}, u32[]{:S(2)}) copy-start(bf16[1,1,6,512,512]{4,3,2,1,0:T(8,128)(2,1)} %param.6) | copy-start | bytes 9437188
  0.0 9.9 %collective-permute-start.1 = (bf16[512,128]{1,0:T(8,128)(2,1)}, bf16[512,128]{1,0:T(8,128)(2,1)S(1)}, u32[]{:S(2)}, u32[]{:S(2)}) collective-permute-start(bf16[512,128]{1,0:T(8,128)(2,1)} %param.5), channel_id=1, source_target_pairs={{451,82},{449,64},{453,493},{455,511},{68,100},{70,118},{66,210},{... | collective-permute-start | bytes 393224 | tf_op jit(solution)/shard_map/ppermute | solution.py:94
  3.1 11.6 %collective-permute-start = (bf16[512,128]{1,0:T(8,128)(2,1)}, bf16[512,128]{1,0:T(8,128)(2,1)S(1)}, u32[]{:S(2)}, u32[]{:S(2)}) collective-permute-start(bf16[512,128]{1,0:T(8,128)(2,1)} %param.5), channel_id=1, source_target_pairs={{387,82},{385,64},{389,493},{391,511},{4,100},{6,118},{2,210},{0,1... | collective-permute-start | bytes 393224 | tf_op jit(solution)/shard_map/ppermute | solution.py:94
  14.9 42.6 %copy-start.1 = (bf16[128,128]{1,0:T(8,128)(2,1)S(1)}, bf16[128,128]{1,0:T(8,128)(2,1)}, u32[]{:S(2)}) copy-start(bf16[128,128]{1,0:T(8,128)(2,1)} %weight.1) | copy-start | bytes 98308
  14.9 42.5 %copy-start.3 = (bf16[128]{0:T(256)(128)(2,1)S(1)}, bf16[128]{0:T(256)(128)(2,1)}, u32[]{:S(2)}) copy-start(bf16[128]{0:T(256)(128)(2,1)} %param.9) | copy-start | bytes 772

commit v5 on v4

--- a/solution.py
+++ b/solution.py
@@ -9,7 +9,7 @@
 from jax.sharding import PartitionSpec as P
 
 SIDE, RING, LINE = 4, 16, 8
-REDUCE_ORDER = 1, 0, 3, 2, 5, 4, 7, 6
+REDUCE_ORDER = 1, 0, 7, 6, 5, 4, 3, 2
 
 
 def device(x, y, z, core):

time: 58.4 us -> 58.3 us (level)
  no operation moved by 1% of the time
where the time goes in v5:
time: 58.3 us; the launch traced here: 58 us
  blocking collectives  40.8 us (70%)
  waiting for transfers between devices  9.69 us (17%)
  starting transfers between devices  4.97 us (9%)
  Pallas kernels  2.31 us (4%)
    all_to_all x1, blocking collectives, local(): lax.all_to_all(partial, 'rep', 0, 0, axis_index_groups=[list(REDUCE_ORDER)])  27.6 us
    all_to_all x1, blocking collectives, local(): lax.all_to_all(jnp.broadcast_to(held[None], (len(groups[0]),) + held.shap...  13.3 us
    ppermute x2, waiting for transfers between devices, local(): lax.ppermute(features, axes, pairs)  9.69 us
    ppermute x2, starting transfers between devices, local(): lax.ppermute(features, axes, pairs)  4.97 us
    pallas_call x1, Pallas kernels, local(): pl.pallas_call(aggregate_kernel, out_shape=jax.ShapeDtypeStruct((replicas...  1.56 us
  transfers between devices with their start and end apart: 2, of which 2 were waited for; matrix products, arithmetic and copies ran while one was open for 0% of the time, Pallas kernels for 0%

profile of v5, /device:TPU:448, one launch (start us, length us, event | category | flops | bytes accessed | tf_op | source)
XLA Modules:
  0.0 58.0 jit_solution(3626556022404878531)
XLA Ops:
  0.0 0.0 copy-start.2
  0.0 0.0 copy-start
  0.0 3.0 %collective-permute-start.1 = (bf16[512,128]{1,0:T(8,128)(2,1)}, bf16[512,128]{1,0:T(8,128)(2,1)S(1)}, u32[]{:S(2)}, u32[]{:S(2)}) collective-permute-start(bf16[512,128]{1,0:T(8,128)(2,1)} %param.5), channel_id=1, source_target_pairs={{451,82},{449,64},{453,493},{455,511},{68,100},{70,118},{66,210},{... | collective-permute-start | bytes 393224 | tf_op jit(solution)/shard_map/ppermute | solution.py:94
  3.1 1.9 %collective-permute-start = (bf16[512,128]{1,0:T(8,128)(2,1)}, bf16[512,128]{1,0:T(8,128)(2,1)S(1)}, u32[]{:S(2)}, u32[]{:S(2)}) collective-permute-start(bf16[512,128]{1,0:T(8,128)(2,1)} %param.5), channel_id=1, source_target_pairs={{387,82},{385,64},{389,493},{391,511},{4,100},{6,118},{2,210},{0,1... | collective-permute-start | bytes 393224 | tf_op jit(solution)/shard_map/ppermute | solution.py:94
  5.0 4.9 %collective-permute-done.1 = bf16[512,128]{1,0:T(8,128)(2,1)S(1)} collective-permute-done((bf16[512,128]{1,0:T(8,128)(2,1)}, bf16[512,128]{1,0:T(8,128)(2,1)S(1)}, u32[]{:S(2)}, u32[]{:S(2)}) %collective-permute-start.1) | collective-permute-done | bytes 131104 | tf_op jit(solution)/shard_map/ppermute | solution.py:94
  9.9 4.8 %collective-permute-done = bf16[512,128]{1,0:T(8,128)(2,1)S(1)} collective-permute-done((bf16[512,128]{1,0:T(8,128)(2,1)}, bf16[512,128]{1,0:T(8,128)(2,1)S(1)}, u32[]{:S(2)}, u32[]{:S(2)}) %collective-permute-start) | collective-permute-done | bytes 131104 | tf_op jit(solution)/shard_map/ppermute | solution.py:94
  14.7 0.1 broadcast_in_dim.2
  14.9 0.0 copy-start.1
  14.9 0.0 copy-start.3
  14.9 13.3 %all_to_all.10 = bf16[4,2,512,128]{3,2,1,0:T(8,128)(2,1)S(1)} all-to-all(bf16[4,2,512,128]{3,2,1,0:T(8,128)(2,1)S(1)} %broadcast_in_dim.2), channel_id=1, replica_groups={{82,100,146,164},{64,118,128,182},{210,228,274,292},{192,246,256,310},{..., dimensions={0} | all-to-all | bytes 2097152 | tf_op jit(solution)/shard_map/all_to_all | solution.py:95
  28.1 0.0 copy-done.2
  28.1 0.0 copy-done
  28.1 1.6 %shard_map.55 = bf16[8,64,128]{2,1,0:T(8,128)(2,1)S(1)} custom-call(s32[6]{0:T(128)S(1)} %bitcast.8, bf16[6,512,512]{2,1,0:T(8,128)(2,1)S(1)} %bitcast.7, bf16[8,512,128]{2,1,0:T(8,128)(2,1)S(1)} %bitcast.6), custom_call_target="tpu_custom_call" | custom-call | tf_op jit(solution)/shard_map/pallas_call | solution.py:99
  29.7 27.6 %all_to_all.11.parts = bf16[8,64,128]{2,1,0:T(8,128)(2,1)S(1)} all-to-all(bf16[8,64,128]{2,1,0:T(8,128)(2,1)S(1)} %shard_map.55), channel_id=1, replica_groups={{1,0,7,6,5,4,3,2},{9,8,15,14,13,12,11,10},{17,16,23,22,21,20,19,18},{25..., dimensions={0} | all-to-all | bytes 262144 | tf_op jit(solution)/shard_map/all_to_all | solution.py:106
  57.3 0.0 copy-done.1
  57.3 0.0 copy-done.3
  57.3 0.8 %shard_map.56 = bf16[64,128]{1,0:T(8,128)(2,1)} custom-call(bf16[8,64,128]{2,1,0:T(8,128)(2,1)S(1)} %all_to_all.11.parts, bf16[128,128]{1,0:T(8,128)(2,1)S(1)} %copy-done.1, bf16[1,128]{1,0:T(2,128)(2,1)S(1)} %bitcast.9), custom_call_target="tpu_custom_call" | custom-call | tf_op jit(solution)/shard_map/pallas_call | solution.py:107
  (1 shorter events, 0.0 us)
Async XLA Ops:
  0.0 28.1 %copy-start.2 = (s32[1,1,6]{2,1,0:T(1,128)S(1)}, s32[1,1,6]{2,1,0:T(1,128)}, u32[]{:S(2)}) copy-start(s32[1,1,6]{2,1,0:T(1,128)} %param.7) | copy-start | bytes 76
  0.0 28.1 %copy-start = (bf16[1,1,6,512,512]{4,3,2,1,0:T(8,128)(2,1)S(1)}, bf16[1,1,6,512,512]{4,3,2,1,0:T(8,128)(2,1)}, u32[]{:S(2)}) copy-start(bf16[1,1,6,512,512]{4,3,2,1,0:T(8,128)(2,1)} %param.6) | copy-start | bytes 9437188
  0.0 9.9 %collective-permute-start.1 = (bf16[512,128]{1,0:T(8,128)(2,1)}, bf16[512,128]{1,0:T(8,128)(2,1)S(1)}, u32[]{:S(2)}, u32[]{:S(2)}) collective-permute-start(bf16[512,128]{1,0:T(8,128)(2,1)} %param.5), channel_id=1, source_target_pairs={{451,82},{449,64},{453,493},{455,511},{68,100},{70,118},{66,210},{... | collective-permute-start | bytes 393224 | tf_op jit(solution)/shard_map/ppermute | solution.py:94
  3.1 11.6 %collective-permute-start = (bf16[512,128]{1,0:T(8,128)(2,1)}, bf16[512,128]{1,0:T(8,128)(2,1)S(1)}, u32[]{:S(2)}, u32[]{:S(2)}) collective-permute-start(bf16[512,128]{1,0:T(8,128)(2,1)} %param.5), channel_id=1, source_target_pairs={{387,82},{385,64},{389,493},{391,511},{4,100},{6,118},{2,210},{0,1... | collective-permute-start | bytes 393224 | tf_op jit(solution)/shard_map/ppermute | solution.py:94
  14.9 42.4 %copy-start.1 = (bf16[128,128]{1,0:T(8,128)(2,1)S(1)}, bf16[128,128]{1,0:T(8,128)(2,1)}, u32[]{:S(2)}) copy-start(bf16[128,128]{1,0:T(8,128)(2,1)} %weight.1) | copy-start | bytes 98308
  14.9 42.4 %copy-start.3 = (bf16[128]{0:T(256)(128)(2,1)S(1)}, bf16[128]{0:T(256)(128)(2,1)}, u32[]{:S(2)}) copy-start(bf16[128]{0:T(256)(128)(2,1)} %param.9) | copy-start | bytes 772
